TPU v7x, 32 devices: a whole 2x2x4 slice. The times are simulated.
32 devices in a mesh: dp: 4 (over z), tensor: 4 (over y, core), pipe: 2 (over x).
Axes of the slice: x: 2, y: 2, z: 4, core: 2. Of those that a mesh axis runs over, the one named last changes fastest.
Arguments:
- normed: bfloat16 [2, 1792, 16384], P('pipe', 'dp', 'tensor'), may hold values from -0.875 to 0.875
- w_value: bfloat16 [2, 16384, 1024], P('pipe', 'tensor'), may hold values from -0.5 to 0.5
- grad_value: bfloat16 [2, 1792, 1024], P('pipe', 'dp'), may hold values from -114688 to 114688
- assistant_mask: int32 [4, 4, 8192], P('dp'), may hold values from 0 to 1, as said below
Outputs:
- value_weight_grad: float32 [2, 4, 4096, 1024], P('pipe', 'tensor', 'dp')
- passed_grad: bfloat16 [2, 1792, 16384], P('pipe', 'dp', 'tensor')
Inputs may be any that keep to these rules, and one draw needn't show every extreme that they name: `assistant_mask`: assistant tokens come in runs of whole turns; every packed sequence holds at least one assistant token.
All inputs are finite; a program needn't handle non-finite values.
Results may differ from a plain program's by a relative error of at most 0.015.
Values may be sent and summed in bfloat16 or wider, within the bound.
A program may use at most 64 MiB of HBM per device.

v0:
```python
import jax
import jax.numpy as jnp
from jax import lax
from jax.sharding import PartitionSpec as P

HEAD = 128
KV_HEADS = 8


def from_behind(block, axis, distance):
    devices = range(lax.axis_size(axis))
    route = [(i - distance, i) for i in devices if i - distance in devices]
    return lax.ppermute(block, axis, route)


def local(normed, w_value, grad_value, assistant_mask):
    local_count = jnp.sum(assistant_mask, dtype=jnp.int32)
    mask_total = lax.psum(local_count, "dp")
    divisor = mask_total.astype(jnp.float32)
    inputs = normed[0]
    weight = w_value[0]
    upstream = grad_value[0]
    local_width = inputs.shape[1]
    replicas = lax.axis_size("dp")
    padded_rows = (local_width + replicas - 1) // replicas * replicas
    padded = jnp.pad(inputs, ((0, 0), (0, padded_rows - local_width)))
    weight_sum = lax.psum_scatter(
        lax.dot_general(
            padded, upstream, (((0,), (0,)), ((), ())), preferred_element_type=jnp.float32
        ).astype(jnp.bfloat16),
        "dp",
        scatter_dimension=0,
        tiled=True,
    ).astype(jnp.float32)
    total = jnp.zeros((upstream.shape[0], local_width), jnp.float32)
    for head in range(KV_HEADS):
        piece_up = upstream[:, head * HEAD : (head + 1) * HEAD]
        piece_w = weight[:, head * HEAD : (head + 1) * HEAD]
        part = lax.dot_general(
            piece_up, piece_w, (((1,), (1,)), ((), ())), preferred_element_type=jnp.float32
        ).astype(jnp.bfloat16)
        total = total + part.astype(jnp.float32)
    weight_grad = weight_sum / divisor
    input_grad = (total / divisor).astype(jnp.bfloat16)
    passed = from_behind(input_grad, "pipe", -1)
    return (weight_grad[None, None], passed[None])


def solution(mesh):
    return jax.shard_map(
        local,
        mesh=mesh,
        in_specs=(
            P("pipe", "dp", "tensor"),
            P("pipe", "tensor", None),
            P("pipe", "dp", None),
            P("dp", None, None),
        ),
        out_specs=(P("pipe", "tensor", "dp", None), P("pipe", "dp", "tensor")),
        check_vma=False,
    )
```

profile of v0, /device:TPU:0, one launch (start us, length us, event | category | flops | bytes accessed | tf_op | source)
XLA Modules:
  0.0 180.0 jit_solution(15836823208902802422)
XLA Ops:
  7.2 0.0 reduce-scatter.2.cloned.1.call-start
  7.2 10.1 %convolution_convert_fusion = bf16[4096,1024]{1,0:T(8,128)(2,1)} fusion(bf16[1,448,4096]{2,1,0:T(8,128)(2,1)} %param.4, bf16[1,448,1024]{2,1,0:T(8,128)(2,1)} %param.6), kind=kOutput, calls=%fused_computation | convolution fusion | flops 3762290688 | bytes 12976128 | tf_op jit(solution)/shard_map/dot_general | solution.py:28
  17.3 0.0 reduce-scatter.2.cloned.1.call-update
  17.3 0.9 copy-done.1
  18.2 0.7 reduce_sum.9
  18.9 10.6 %psum.7 = s32[]{:T(128)} all-reduce(s32[]{:T(128)} %reduce_sum.9), channel_id=1, replica_groups=mesh['dp'=4,'tensor'=4,'pipe'=2] {'dp'}, use_global_device_ids=true, to_apply=%region_2.3 | all-reduce | flops 1 | bytes 8 | tf_op jit(solution)/shard_map/psum | solution.py:18
  30.2 0.0 copy-done
  30.2 0.0 slice-start
  30.2 2.5 %convolution_convert_fusion.1 = bf16[448,4096]{1,0:T(8,128)(2,1)S(1)} fusion(bf16[4096,1024]{1,0:T(8,128)(2,1)} %bitcast.10, bf16[448,1024]{1,0:T(8,128)(2,1)S(1)} %bitcast.20), kind=kOutput, calls=%fused_computation.2 | convolution fusion | flops 471597056 | bytes 4833280 | tf_op jit(solution)/shard_map/dot_general | solution.py:39
  32.7 0.0 slice-start.1
  32.7 2.5 %convolution_convert_fusion.2 = bf16[448,4096]{1,0:T(8,128)(2,1)S(1)} fusion(bf16[4096,1024]{1,0:T(8,128)(2,1)} %bitcast.11, bf16[448,1024]{1,0:T(8,128)(2,1)S(1)} %bitcast.21), kind=kOutput, calls=%fused_computation.3 | convolution fusion | flops 471597056 | bytes 4833280 | tf_op jit(solution)/shard_map/dot_general | solution.py:39
  35.2 2.4 %convolution_convert_fusion.3 = bf16[448,4096]{1,0:T(8,128)(2,1)S(1)} fusion(bf16[4096,1024]{1,0:T(8,128)(2,1)} %bitcast.12, bf16[448,1024]{1,0:T(8,128)(2,1)S(1)} %bitcast.22), kind=kOutput, calls=%fused_computation.4 | convolution fusion | flops 471597056 | bytes 4833280 | tf_op jit(solution)/shard_map/dot_general | solution.py:39
  37.6 0.0 slice-done
  37.6 0.0 slice-done.1
  37.6 1.1 convolution_convert_fusion.4
  38.7 3.0 %convolution_convert_fusion.5 = bf16[448,4096]{1,0:T(8,128)(2,1)} fusion(bf16[4096,1024]{1,0:T(8,128)(2,1)S(1)} %bitcast.17, bf16[448,1024]{1,0:T(8,128)(2,1)S(1)} %bitcast.24), kind=kOutput, calls=%fused_computation.6 | convolution fusion | flops 471597056 | bytes 4833280 | tf_op jit(solution)/shard_map/dot_general | solution.py:39
  41.7 3.0 %convolution_convert_fusion.6 = bf16[448,4096]{1,0:T(8,128)(2,1)} fusion(bf16[4096,1024]{1,0:T(8,128)(2,1)S(1)} %bitcast.18, bf16[448,1024]{1,0:T(8,128)(2,1)S(1)} %bitcast.25), kind=kOutput, calls=%fused_computation.7 | convolution fusion | flops 471597056 | bytes 4833280 | tf_op jit(solution)/shard_map/dot_general | solution.py:39
  44.7 3.0 %convolution_convert_fusion.7 = bf16[448,4096]{1,0:T(8,128)(2,1)} fusion(bf16[4096,1024]{1,0:T(8,128)(2,1)S(1)} %bitcast.19, bf16[448,1024]{1,0:T(8,128)(2,1)S(1)} %bitcast.26), kind=kOutput, calls=%fused_computation.8 | convolution fusion | flops 471597056 | bytes 4833280 | tf_op jit(solution)/shard_map/dot_general | solution.py:39
  47.7 9.3 %divide_convert_fusion = bf16[448,4096]{1,0:T(8,128)(2,1)} fusion(bf16[448,4096]{1,0:T(8,128)(2,1)S(1)} %convolution_convert_fusion.1, bf16[448,4096]{1,0:T(8,128)(2,1)S(1)} %convolution_convert_fusion.2, bf16[448,4096]{1,0:T(8,128)(2,1)S(1)} %convolution_convert_fusion.3, bf16[448,4096]{1,0:T(8,128)(2,1)S(1)} %convolution_convert_fusion.4, ...), kind=kOutput, calls=%fused_computation.1 | convolution fusion | flops 502792192 | bytes 30523396 | tf_op jit(solution)/shard_map/dot_general | solution.py:39
  57.0 1.3 collective-permute-start
  58.3 79.9 %collective-permute-done = bf16[448,4096]{1,0:T(8,128)(2,1)} collective-permute-done((bf16[448,4096]{1,0:T(8,128)(2,1)}, bf16[448,4096]{1,0:T(8,128)(2,1)}, u32[]{:S(2)}, u32[]{:S(2)}) %collective-permute-start) | collective-permute-done | bytes 3670048 | tf_op jit(solution)/shard_map/ppermute | solution.py:13
  138.2 26.4 %reduce-scatter.2.cloned.1.call-done = bf16[1024,1024]{1,0:T(8,128)(2,1)} async-done(((bf16[4096,1024]{1,0:T(8,128)(2,1)}), bf16[1024,1024]{1,0:T(8,128)(2,1)}) %reduce-scatter.2.cloned.1.call-update) | async-done | bytes 2097168 | tf_op jit(solution)/shard_map/reduce_scatter | solution.py:27
  164.6 4.2 %divide_bitcast_fusion = f32[1,1,1024,1024]{3,2,1,0:T(8,128)} fusion(bf16[1024,1024]{1,0:T(8,128)(2,1)} %reduce-scatter.2.cloned.1.call-done, f32[]{:T(128)S(6)} %convert_element_type.62), kind=kLoop, calls=%fused_computation.10 | loop fusion | flops 2097152 | bytes 6291460 | tf_op jit(solution)/shard_map/broadcast_in_dim | solution.py:46
  168.8 4.3 %copy.7 = bf16[1,448,4096]{2,1,0:T(8,128)(2,1)} copy(bf16[1,448,4096]{2,1,0:T(8,128)(2,1)} %bitcast.4) | data formatting | bytes 7340032
  (3 shorter events, 0.0 us)
Async XLA Ops:
  7.2 157.4 %reduce-scatter.2.cloned.1.call-start = ((), (), s32[]{:S(2)}) async-start(), calls=%async_computation.1 | async-start | bytes 10485760 | tf_op jit(solution)/shard_map/reduce_scatter | solution.py:27
  17.3 0.9 copy-start.1
  17.3 12.9 %copy-start = (bf16[1,448,1024]{2,1,0:T(8,128)(2,1)S(1)}, bf16[1,448,1024]{2,1,0:T(8,128)(2,1)}, u32[]{:S(2)}) copy-start(bf16[1,448,1024]{2,1,0:T(8,128)(2,1)} %param.6) | copy-start | bytes 2752516
  30.2 7.4 %slice-start = ((s8[8388608]{0:T(1024)(128)(4,1)}), s8[4194304]{0:T(1024)(128)(4,1)S(1)}, s32[]{:S(2)}) async-start(s8[8388608]{0:T(1024)(128)(4,1)} %bitcast.14), calls=%async_computation.2 | async-start | bytes 8388608
  32.7 4.9 %slice-start.1 = ((s8[8388608]{0:T(1024)(128)(4,1)}), s8[4194304]{0:T(1024)(128)(4,1)S(1)}, s32[]{:S(2)}) async-start(s8[8388608]{0:T(1024)(128)(4,1)} %bitcast.14), calls=%async_computation.3 | async-start | bytes 8388608
  57.0 81.2 %collective-permute-start = (bf16[448,4096]{1,0:T(8,128)(2,1)}, bf16[448,4096]{1,0:T(8,128)(2,1)}, u32[]{:S(2)}, u32[]{:S(2)}) collective-permute-start(bf16[448,4096]{1,0:T(8,128)(2,1)} %divide_convert_fusion), channel_id=1, source_target_pairs={{1,0},{3,2},{5,4},{7,6},{9,8},{11,10},{13,12},{15,14},{17,16},{19,... | collective-permute-start | bytes 11010056 | tf_op jit(solution)/shard_map/ppermute | solution.py:13
Sparse Core Ops, SparseCore 0:
  17.4 147.1 reduce-scatter.1
where the time goes:
time: 180 us
  waiting for transfers between devices  106 us (59%)
  matrix products  36.8 us (20%)
  between operations  14.8 us (8%)
  blocking collectives  10.6 us (6%)
  local copies, waits for them, and re-layouts  5.19 us (3%)
  other arithmetic  4.91 us (3%)
    ppermute x1, waiting for transfers between devices, from_behind(): return lax.ppermute(block, axis, route)  79.9 us
    dot_general x8, matrix products, local(): lax.dot_general(piece_up, piece_w, (((1,), (1,)), ((), ())), preferred_el...  26.8 us
    reduce_scatter x1, waiting for transfers between devices, local(): lax.psum_scatter(lax.dot_general(padded, upstream, (((0,), (0,)), ((), ()...  26.4 us
    psum x1, blocking collectives, local(): mask_total = lax.psum(local_count, 'dp')  10.6 us
    dot_general x1, matrix products, local(): lax.dot_general(padded, upstream, (((0,), (0,)), ((), ())), preferred_ele...  10.1 us
    unnamed x9, local copies, waits for them, and re-layouts  5.19 us
    broadcast_in_dim x1, other arithmetic, local(): return (weight_grad[None, None], passed[None])  4.21 us
  transfers between devices with their start and end apart: 2, of which 2 were waited for; matrix products, arithmetic and copies ran while one was open for 15% of the time, Pallas kernels for 0%

commit v1 on v0

--- a/solution.py
+++ b/solution.py
@@ -1,10 +1,17 @@
+import functools
+
 import jax
 import jax.numpy as jnp
 from jax import lax
+from jax.experimental import pallas as pl
+from jax.experimental.pallas import tpu as pltpu
 from jax.sharding import PartitionSpec as P
 
 HEAD = 128
 KV_HEADS = 8
+LANES = 128
+PACK = 16
+MESH = pl.DeviceIdType.MESH
 
 
 def from_behind(block, axis, distance):
@@ -13,7 +20,298 @@
     return lax.ppermute(block, axis, route)
 
 
-def local(normed, w_value, grad_value, assistant_mask):
+def pieces_of(extent, unit, most):
+    for count in range(most, 0, -1):
+        if extent % (count * unit) == 0:
+            return count
+    return 1
+
+
+def exchange(
+    replicas, tensors, sections, x_cuts, w_cuts,
+    normed, weight, grad, mask,
+    total, passed, count,
+    mine, arrived, grads, weights, sending, counts,
+    load_sem, w_sem, n_send, n_recv, g_send, g_recv, f_send, f_recv, c_send, c_recv, x_send, x_recv,
+):
+    dp = lax.axis_index("dp")
+    tensor = lax.axis_index("tensor")
+    pipe = lax.axis_index("pipe")
+    rows = grads.shape[1]
+    share = rows // tensors
+    owned = mine.shape[1]
+    step = passed.shape[1] // x_cuts
+
+    def peer(d):
+        return lax.rem(dp + d, replicas)
+
+    def mate(e):
+        return lax.rem(tensor + e, tensors)
+
+    def part(index):
+        return pl.ds(pl.multiple_of(index * share, PACK), share)
+
+    def columns(index):
+        return pl.ds(pl.multiple_of(index * owned, LANES), owned)
+
+    grad_load = pltpu.make_async_copy(grad.at[0], grads.at[0], load_sem.at[0])
+    grad_load.start()
+    w_loads = [
+        pltpu.make_async_copy(
+            weight.at[0, pl.ds(c * step, step)], weights.at[pl.ds(c * step, step)], w_sem.at[c]
+        )
+        for c in range(x_cuts)
+    ]
+
+    @pl.when(pipe > 0)
+    def _():
+        for load in w_loads:
+            load.start()
+
+    mine_load = pltpu.make_async_copy(normed.at[0, :, columns(dp)], mine, load_sem.at[1])
+    mine_load.start()
+
+    barrier = pltpu.get_barrier_semaphore()
+    for d in range(1, replicas):
+        pl.semaphore_signal(barrier, inc=1, device_id={"dp": peer(d)}, device_id_type=MESH)
+    for e in range(1, tensors):
+        pl.semaphore_signal(barrier, inc=1, device_id={"tensor": mate(e)}, device_id_type=MESH)
+
+    pl.semaphore_signal(
+        barrier, inc=1, device_id={"pipe": lax.rem(pipe + 1, sections)}, device_id_type=MESH
+    )
+    pl.semaphore_wait(barrier, replicas - 1 + tensors - 1 + 1)
+
+    g_copies = [
+        pltpu.make_async_remote_copy(
+            src_ref=grad.at[0, part(tensor)],
+            dst_ref=grads.at[d, part(tensor)],
+            send_sem=g_send.at[d],
+            recv_sem=g_recv.at[d],
+            device_id={"dp": peer(d)},
+            device_id_type=MESH,
+        )
+        for d in range(1, replicas)
+    ]
+    n_copies = [
+        pltpu.make_async_remote_copy(
+            src_ref=normed.at[0, :, columns(peer(d))],
+            dst_ref=arrived.at[d - 1],
+            send_sem=n_send.at[d],
+            recv_sem=n_recv.at[d],
+            device_id={"dp": peer(d)},
+            device_id_type=MESH,
+        )
+        for d in range(1, replicas)
+    ]
+    for copy in g_copies:
+        copy.start()
+    for copy in n_copies:
+        copy.start()
+
+    grad_load.wait()
+
+    def x_copy(c):
+        cut = pl.ds(c * step, step)
+        return pltpu.make_async_remote_copy(
+            src_ref=sending.at[:, cut],
+            dst_ref=passed.at[:, cut],
+            send_sem=x_send.at[c],
+            recv_sem=x_recv.at[c],
+            device_id={"pipe": lax.rem(pipe + sections - 1, sections)},
+            device_id_type=MESH,
+        )
+
+    @pl.when(pipe > 0)
+    def _():
+        for c in range(x_cuts):
+            w_loads[c].wait()
+            sending[:, c * step : (c + 1) * step] = lax.dot_general(
+                grads[0],
+                weights[c * step : (c + 1) * step, :],
+                (((1,), (1,)), ((), ())),
+                preferred_element_type=jnp.float32,
+            ).astype(sending.dtype)
+            x_copy(c).start()
+
+    counts[0] = jnp.full(counts.shape[1:], jnp.sum(mask[...], dtype=jnp.int32), jnp.int32)
+    c_copies = [
+        pltpu.make_async_remote_copy(
+            src_ref=counts.at[0],
+            dst_ref=counts.at[d],
+            send_sem=c_send.at[d],
+            recv_sem=c_recv.at[d],
+            device_id={"dp": peer(d)},
+            device_id_type=MESH,
+        )
+        for d in range(1, replicas)
+    ]
+    for copy in c_copies:
+        copy.start()
+
+    def forward(d, e):
+        return pltpu.make_async_remote_copy(
+            src_ref=grads.at[d, part(tensor)],
+            dst_ref=grads.at[d, part(tensor)],
+            send_sem=f_send.at[d, e],
+            recv_sem=f_recv.at[d, e],
+            device_id={"tensor": mate(e)},
+            device_id_type=MESH,
+        )
+
+    forwards = [[forward(d, e) for e in range(1, tensors)] for d in range(1, replicas)]
+    for d in range(1, replicas):
+        g_copies[d - 1].wait_recv()
+        for copy in forwards[d - 1]:
+            copy.start()
+
+    tile = owned // w_cuts
+
+    def add(d, block):
+        for k in range(w_cuts):
+            cut = slice(k * tile, (k + 1) * tile)
+            product = lax.dot_general(
+                block[:, cut], grads[d], (((0,), (0,)), ((), ())), preferred_element_type=jnp.float32
+            )
+            if d == 0:
+                total[cut, :] = product
+            else:
+                total[cut, :] += product
+
+    mine_load.wait()
+    add(0, mine)
+    for copy in c_copies:
+        copy.wait()
+    whole = counts[0]
+    for d in range(1, replicas):
+        whole = whole + counts[d]
+    count[...] = whole.astype(jnp.float32)
+    for d in range(1, replicas):
+        for copy in forwards[d - 1]:
+            copy.wait_recv()
+        n_copies[d - 1].wait_recv()
+        add(d, arrived.at[d - 1])
+
+    @pl.when(pipe < sections - 1)
+    def _():
+        for c in range(x_cuts):
+            x_copy(c).wait_recv()
+
+    @pl.when(pipe > 0)
+    def _():
+        for c in range(x_cuts):
+            x_copy(c).wait_send()
+
+    for d in range(1, replicas):
+        g_copies[d - 1].wait_send()
+        n_copies[d - 1].wait_send()
+        for copy in forwards[d - 1]:
+            copy.wait_send()
+
+
+def finish(sections, cuts, total, passed, count, grad_out, passed_out, grad_part, passed_part, g_sem, p_sem):
+    pipe = lax.axis_index("pipe")
+    divisor = count[0:1, 0:1]
+    high = total.shape[0] // cuts
+    wide = passed.shape[1] // cuts
+    copies = []
+    for c in range(cuts):
+        tall = slice(c * high, (c + 1) * high)
+        cut = slice(c * wide, (c + 1) * wide)
+        grad_part[tall, :] = total[tall, :] / divisor
+        copy = pltpu.make_async_copy(
+            grad_part.at[pl.ds(c * high, high)], grad_out.at[0, 0, pl.ds(c * high, high)], g_sem.at[c]
+        )
+        copy.start()
+        copies.append(copy)
+
+        @pl.when(pipe < sections - 1)
+        def _():
+            passed_part[:, cut] = (passed[:, cut].astype(jnp.float32) / divisor).astype(passed_part.dtype)
+
+        @pl.when(pipe == sections - 1)
+        def _():
+            passed_part[:, cut] = jnp.zeros((passed.shape[0], wide), passed_part.dtype)
+
+        copy = pltpu.make_async_copy(
+            passed_part.at[:, pl.ds(c * wide, wide)], passed_out.at[0, :, pl.ds(c * wide, wide)], p_sem.at[c]
+        )
+        copy.start()
+        copies.append(copy)
+    for copy in copies:
+        copy.wait()
+
+
+def in_kernels(replicas, tensors, sections, normed, w_value, grad_value, assistant_mask):
+    _, rows, width = normed.shape
+    heads = w_value.shape[2]
+    owned = width // replicas
+    x_cuts = pieces_of(width, LANES, 8)
+    w_cuts = pieces_of(owned, LANES, 4)
+    out_cuts = pieces_of(owned, LANES, 4)
+    kind = normed.dtype
+    vmem = pl.BlockSpec(memory_space=pltpu.VMEM)
+    anywhere = pl.BlockSpec(memory_space=pl.ANY)
+    dma = pltpu.SemaphoreType.DMA
+    size = kind.itemsize
+    held = size * (rows * owned * replicas + replicas * rows * heads + width * heads + rows * width)
+    held += 4 * assistant_mask.size + 4 * owned * heads + size * rows * width
+    total, passed, count = pl.pallas_call(
+        functools.partial(exchange, replicas, tensors, sections, x_cuts, w_cuts),
+        out_shape=(
+            pltpu.VMEM((owned, heads), jnp.float32),
+            pltpu.VMEM((rows, width), kind),
+            pltpu.VMEM((8, LANES), jnp.float32),
+        ),
+        in_specs=[anywhere, anywhere, anywhere, vmem],
+        out_specs=(vmem, vmem, vmem),
+        scratch_shapes=[
+            pltpu.VMEM((rows, owned), kind),
+            pltpu.VMEM((replicas - 1, rows, owned), kind),
+            pltpu.VMEM((replicas, rows, heads), kind),
+            pltpu.VMEM((width, heads), kind),
+            pltpu.VMEM((rows, width), kind),
+            pltpu.VMEM((replicas, 8, LANES), jnp.int32),
+            dma((2,)),
+            dma((x_cuts,)),
+            dma((replicas,)),
+            dma((replicas,)),
+            dma((replicas,)),
+            dma((replicas,)),
+            dma((replicas, tensors)),
+            dma((replicas, tensors)),
+            dma((replicas,)),
+            dma((replicas,)),
+            dma((x_cuts,)),
+            dma((x_cuts,)),
+        ],
+        compiler_params=pltpu.CompilerParams(
+            collective_id=0, has_side_effects=True, vmem_limit_bytes=held + (8 << 20)
+        ),
+        name="exchange",
+    )(normed, w_value, grad_value, assistant_mask)
+    return pl.pallas_call(
+        functools.partial(finish, sections, out_cuts),
+        out_shape=(
+            jax.ShapeDtypeStruct((1, 1, owned, heads), jnp.float32),
+            jax.ShapeDtypeStruct((1, rows, width), kind),
+        ),
+        in_specs=[vmem, vmem, vmem],
+        out_specs=(anywhere, anywhere),
+        scratch_shapes=[
+            pltpu.VMEM((owned, heads), jnp.float32),
+            pltpu.VMEM((rows, width), kind),
+            dma((out_cuts,)),
+            dma((out_cuts,)),
+        ],
+        compiler_params=pltpu.CompilerParams(
+            vmem_limit_bytes=2 * (4 * owned * heads + size * rows * width) + (8 << 20)
+        ),
+        name="finish",
+    )(total, passed, count)
+
+
+def with_collectives(normed, w_value, grad_value, assistant_mask):
     local_count = jnp.sum(assistant_mask, dtype=jnp.int32)
     mask_total = lax.psum(local_count, "dp")
     divisor = mask_total.astype(jnp.float32)
@@ -47,6 +345,15 @@
 
 
 def solution(mesh):
+    replicas, tensors, sections = mesh.shape["dp"], mesh.shape["tensor"], mesh.shape["pipe"]
+
+    def local(normed, w_value, grad_value, assistant_mask):
+        _, rows, width = normed.shape
+        aligned = width % (replicas * LANES) == 0 and rows % (tensors * PACK) == 0
+        if aligned and min(replicas, tensors, sections) > 1:
+            return in_kernels(replicas, tensors, sections, normed, w_value, grad_value, assistant_mask)
+        return with_collectives(normed, w_value, grad_value, assistant_mask)
+
     return jax.shard_map(
         local,
         mesh=mesh,

time: 180 us -> 119 us (0.66)
  Pallas kernels: 0 us -> 114 us
  waiting for transfers between devices: 106 us -> 0 us
  matrix products: 36.8 us -> 0 us
  between operations: 14.8 us -> 0.65 us
  blocking collectives: 10.6 us -> 0 us
  other arithmetic: 4.91 us -> 0 us
    pallas_call x0 -> x2, Pallas kernels: none -> 114 us  [the longest x1 110 us: in_kernels(): pl.pallas_call(functools.partial(exchange, replicas, tensors, sections, x...]
    ppermute x1 -> x0, waiting for transfers between devices: 79.9 us -> none  [from_behind(): return lax.ppermute(block, axis, route)]
    dot_general x9 -> x0, matrix products: 36.8 us -> none  [the longest x8 26.8 us: local(): lax.dot_general(piece_up, piece_w, (((1,), (1,)), ((), ())), preferred_el...]
    reduce_scatter x1 -> x0, waiting for transfers between devices: 26.4 us -> none  [local(): lax.psum_scatter(lax.dot_general(padded, upstream, (((0,), (0,)), ((), ()...]
    psum x1 -> x0, blocking collectives: 10.6 us -> none  [local(): mask_total = lax.psum(local_count, 'dp')]
    broadcast_in_dim x1 -> x0, other arithmetic: 4.21 us -> none  [local(): return (weight_grad[None, None], passed[None])]
    unnamed x9 -> x6, local copies, waits for them, and re-layouts: 5.19 us -> 4.11 us
  transfers between devices with their start and end apart: 2 -> 0, of which waited for: 2 -> 0; matrix products, arithmetic and copies ran while one was open for 15% -> 0% of each run, Pallas kernels for 0% -> 0%
where the time goes in v1:
time: 119 us; the launch traced here: 118 us
  Pallas kernels  114 us (96%)
  local copies, waits for them, and re-layouts  4.11 us (3%)
    pallas_call x1, Pallas kernels, in_kernels(): pl.pallas_call(functools.partial(exchange, replicas, tensors, sections, x...  110 us
    unnamed x6, local copies, waits for them, and re-layouts  4.11 us
    pallas_call x1, Pallas kernels, in_kernels(): pl.pallas_call(functools.partial(finish, sections, out_cuts), out_shape=(...  3.33 us

profile of v1, /device:TPU:0, one launch (start us, length us, event | category | flops | bytes accessed | tf_op | source)
XLA Modules:
  0.0 118.4 jit_solution(17445026039860043775)
XLA Ops:
  0.6 0.0 copy-start
  0.6 2.0 %copy-done = bf16[1,448,4096]{2,1,0:T(8,128)(2,1)S(1)} copy-done((bf16[1,448,4096]{2,1,0:T(8,128)(2,1)S(1)}, bf16[1,448,4096]{2,1,0:T(8,128)(2,1)}, u32[]{:S(2)}) %copy-start) | copy-done | bytes 3670040
  2.7 0.0 copy-start.1
  2.7 1.2 copy-done.1
  3.8 0.0 copy-start.2
  3.9 0.9 copy-done.2
  4.8 110.3 %exchange.1 = (f32[1024,1024]{1,0:T(8,128)S(1)}, bf16[448,4096]{1,0:T(8,128)(2,1)S(1)}, f32[8,128]{1,0:T(8,128)S(1)}) custom-call(bf16[1,448,4096]{2,1,0:T(8,128)(2,1)S(1)} %copy-done, bf16[1,4096,1024]{2,1,0:T(8,128)(2,1)} %weight.1, bf16[1,448,1024]{2,1,0:T(8,128)(2,1)S(1)} %copy-done.1, s32[1,4,8192]{2,1,0:T(4,128)S(1)} %copy-done.2), custom_call_target="tpu_custom_call" | custom-call | tf_op jit(solution)/shard_map/exchange/pallas_call | solution.py:259
  115.0 3.3 %finish.1 = (f32[1,1,1024,1024]{3,2,1,0:T(8,128)}, bf16[1,448,4096]{2,1,0:T(8,128)(2,1)}) custom-call(f32[1024,1024]{1,0:T(8,128)S(1)} %get-tuple-element.5.total, bf16[448,4096]{1,0:T(8,128)(2,1)S(1)} %get-tuple-element.6.passed, f32[8,128]{1,0:T(8,128)S(1)} %get-tuple-element.7.count), custom_call_target="tpu_custom_call" | custom-call | tf_op jit(solution)/shard_map/finish/pallas_call | solution.py:293
Async XLA Ops:
  0.6 2.0 %copy-start = (bf16[1,448,4096]{2,1,0:T(8,128)(2,1)S(1)}, bf16[1,448,4096]{2,1,0:T(8,128)(2,1)}, u32[]{:S(2)}) copy-start(bf16[1,448,4096]{2,1,0:T(8,128)(2,1)} %normed.1) | copy-start | bytes 11010052
  2.7 1.2 copy-start.1
  3.8 0.9 copy-start.2

commit v2 on v1

v2 whole, which is shorter than its diff:
```python
import functools

import jax
import jax.numpy as jnp
from jax import lax
from jax.experimental import pallas as pl
from jax.experimental.pallas import tpu as pltpu
from jax.sharding import PartitionSpec as P

HEAD = 128
KV_HEADS = 8
LANES = 128
PACK = 16
MESH = pl.DeviceIdType.MESH


def from_behind(block, axis, distance):
    devices = range(lax.axis_size(axis))
    route = [(i - distance, i) for i in devices if i - distance in devices]
    return lax.ppermute(block, axis, route)


def pieces_of(extent, unit, most):
    for count in range(most, 0, -1):
        if extent % (count * unit) == 0:
            return count
    return 1


def exchange(
    replicas, tensors, sections, x_cuts, n_cuts,
    normed, weight, grad, mask,
    total, passed,
    mine, arrived, grads, weights, sending, counts, masks,
    load_sem, w_sem, n_send, n_recv, g_send, g_recv, f_send, f_recv, c_send, c_recv, x_send, x_recv,
):
    dp = lax.axis_index("dp")
    tensor = lax.axis_index("tensor")
    pipe = lax.axis_index("pipe")
    rows = grads.shape[1]
    share = rows // tensors
    owned = mine.shape[1]
    tile = owned // n_cuts
    step = passed.shape[1] // x_cuts
    bits = [1 << b for b in reversed(range(replicas.bit_length() - 1))]
    offsets = range(replicas - 1, 0, -1)

    def peer(d):
        return dp + sum(b * (1 - 2 * lax.rem(dp // b, 2)) for b in bits if d & b)

    def mate(e):
        return lax.rem(tensor + e, tensors)

    def part(index):
        return pl.ds(pl.multiple_of(index * share, PACK), share)

    def columns(index, k):
        return pl.ds(pl.multiple_of(index * owned + k * tile, LANES), tile)

    barrier = pltpu.get_barrier_semaphore()
    for d in offsets:
        pl.semaphore_signal(barrier, inc=1, device_id={"dp": peer(d)}, device_id_type=MESH)
    for e in range(1, tensors):
        pl.semaphore_signal(barrier, inc=1, device_id={"tensor": mate(e)}, device_id_type=MESH)
    pl.semaphore_signal(
        barrier, inc=1, device_id={"pipe": lax.rem(pipe + 1, sections)}, device_id_type=MESH
    )

    grad_load = pltpu.make_async_copy(grad.at[0], grads.at[0], load_sem.at[0])
    grad_load.start()
    w_loads = [
        pltpu.make_async_copy(
            weight.at[0, pl.ds(c * step, step)], weights.at[pl.ds(c * step, step)], w_sem.at[c]
        )
        for c in range(x_cuts)
    ]

    @pl.when(pipe > 0)
    def _():
        for load in w_loads:
            load.start()

    mask_load = pltpu.make_async_copy(mask.at[0], masks, load_sem.at[1])
    mask_load.start()
    mine_load = pltpu.make_async_copy(
        normed.at[0, :, pl.ds(pl.multiple_of(dp * owned, LANES), owned)], mine, load_sem.at[2]
    )
    mine_load.start()

    pl.semaphore_wait(barrier, replicas - 1 + tensors - 1 + 1)

    def g_copy(source, slot, b):
        return pltpu.make_async_remote_copy(
            src_ref=source,
            dst_ref=grads.at[slot + b, part(tensor)],
            send_sem=g_send.at[slot + b],
            recv_sem=g_recv.at[slot + b],
            device_id={"dp": peer(b)},
            device_id_type=MESH,
        )

    def n_copy(d, k):
        return pltpu.make_async_remote_copy(
            src_ref=normed.at[0, :, columns(peer(d), k)],
            dst_ref=arrived.at[d - 1, k],
            send_sem=n_send.at[d, k],
            recv_sem=n_recv.at[d, k],
            device_id={"dp": peer(d)},
            device_id_type=MESH,
        )

    def x_copy(c):
        cut = pl.ds(c * step, step)
        return pltpu.make_async_remote_copy(
            src_ref=sending.at[:, cut],
            dst_ref=passed.at[:, cut],
            send_sem=x_send.at[c],
            recv_sem=x_recv.at[c],
            device_id={"pipe": lax.rem(pipe + sections - 1, sections)},
            device_id_type=MESH,
        )

    def forward(d, e):
        return pltpu.make_async_remote_copy(
            src_ref=grads.at[d, part(tensor)],
            dst_ref=grads.at[d, part(tensor)],
            send_sem=f_send.at[d, e],
            recv_sem=f_recv.at[d, e],
            device_id={"tensor": mate(e)},
            device_id_type=MESH,
        )

    own = grad.at[0, part(tensor)]
    g_copies = {b: g_copy(own, 0, b) for b in bits}
    for b in bits:
        g_copies[b].start()
    ahead = min(2, n_cuts)
    n_copies = {(d, k): n_copy(d, k) for d in offsets for k in range(n_cuts)}
    for k in range(ahead):
        for d in offsets:
            n_copies[d, k].start()

    grad_load.wait()

    @pl.when(pipe > 0)
    def _():
        for c in range(x_cuts):
            w_loads[c].wait()
            sending[:, c * step : (c + 1) * step] = lax.dot_general(
                grads[0],
                weights[c * step : (c + 1) * step, :],
                (((1,), (1,)), ((), ())),
                preferred_element_type=jnp.float32,
            ).astype(sending.dtype)
            x_copy(c).start()

    mask_load.wait()
    counts[0] = jnp.full(counts.shape[1:], jnp.sum(masks[...], dtype=jnp.int32), jnp.int32)
    c_copies = [
        pltpu.make_async_remote_copy(
            src_ref=counts.at[0],
            dst_ref=counts.at[d],
            send_sem=c_send.at[d],
            recv_sem=c_recv.at[d],
            device_id={"dp": peer(d)},
            device_id_type=MESH,
        )
        for d in offsets
    ]
    for copy in c_copies:
        copy.start()

    forwards = {(d, e): forward(d, e) for d in offsets for e in range(1, tensors)}
    held = [0]
    for i, b in enumerate(bits):
        for slot in held:
            g_copies[slot + b].wait_recv()
            for later in bits[i + 1 :]:
                g_copies[slot + b + later] = g_copy(grads.at[slot + b, part(tensor)], slot + b, later)
                g_copies[slot + b + later].start()
            for e in range(1, tensors):
                forwards[slot + b, e].start()
        held = held + [slot + b for slot in held]

    for copy in c_copies:
        copy.wait()
    whole = counts[0]
    for d in offsets:
        whole = whole + counts[d]
    divisor = whole.astype(jnp.float32)[0:1, 0:1]

    def times(block, d):
        return lax.dot_general(
            block, grads[d], (((0,), (0,)), ((), ())), preferred_element_type=jnp.float32
        )

    mine_load.wait()
    for k in range(n_cuts):
        cut = slice(k * tile, (k + 1) * tile)
        total[cut, :] = times(mine[:, cut], 0)
    for d in offsets:
        for e in range(1, tensors):
            forwards[d, e].wait_recv()
    for k in range(n_cuts):
        cut = slice(k * tile, (k + 1) * tile)
        if k + ahead < n_cuts:
            for d in offsets:
                n_copies[d, k].wait_send()
                n_copies[d, k + ahead].start()
        if k == n_cuts - 1:

            @pl.when(pipe < sections - 1)
            def _():
                for c in range(x_cuts):
                    x_copy(c).wait_recv()
                    wide = slice(c * step, (c + 1) * step)
                    passed[:, wide] = (passed[:, wide].astype(jnp.float32) / divisor).astype(passed.dtype)

            @pl.when(pipe == sections - 1)
            def _():
                passed[...] = jnp.zeros(passed.shape, passed.dtype)

            @pl.when(pipe > 0)
            def _():
                for c in range(x_cuts):
                    x_copy(c).wait_send()

        for d in reversed(offsets):
            n_copies[d, k].wait_recv()
            if d == offsets[0]:
                total[cut, :] = (total[cut, :] + times(arrived[d - 1, k], d)) / divisor
            else:
                total[cut, :] += times(arrived[d - 1, k], d)

    for k in range(max(n_cuts - ahead, 0), n_cuts):
        for d in offsets:
            n_copies[d, k].wait_send()
    for d in offsets:
        g_copies[d].wait_send()
        for e in range(1, tensors):
            forwards[d, e].wait_send()


def finish(cuts, total, passed, grad_out, passed_out, g_sem, p_sem):
    high = total.shape[0] // cuts
    wide = passed.shape[1] // cuts
    copies = []
    for c in range(cuts):
        tall, cut = pl.ds(c * high, high), pl.ds(c * wide, wide)
        copies.append(pltpu.make_async_copy(total.at[tall], grad_out.at[0, 0, tall], g_sem.at[c]))
        copies.append(pltpu.make_async_copy(passed.at[:, cut], passed_out.at[0, :, cut], p_sem.at[c]))
    for copy in copies:
        copy.start()
    for copy in copies:
        copy.wait()


def in_kernels(replicas, tensors, sections, normed, w_value, grad_value, assistant_mask):
    _, rows, width = normed.shape
    heads = w_value.shape[2]
    owned = width // replicas
    x_cuts = pieces_of(width, LANES, 8)
    n_cuts = pieces_of(owned, LANES, 4)
    kind = normed.dtype
    vmem = pl.BlockSpec(memory_space=pltpu.VMEM)
    anywhere = pl.BlockSpec(memory_space=pl.ANY)
    dma = pltpu.SemaphoreType.DMA
    size = kind.itemsize
    held = size * (rows * owned * replicas + replicas * rows * heads + width * heads + rows * width)
    held += 4 * assistant_mask.size
    arguments = [
        pltpu.with_memory_space_constraint(array, pltpu.HBM)
        for array in (normed, w_value, grad_value, assistant_mask)
    ]
    total, passed = pl.pallas_call(
        functools.partial(exchange, replicas, tensors, sections, x_cuts, n_cuts),
        out_shape=(
            pltpu.VMEM((owned, heads), jnp.float32),
            pltpu.VMEM((rows, width), kind),
        ),
        in_specs=[anywhere] * 4,
        out_specs=(vmem, vmem),
        scratch_shapes=[
            pltpu.VMEM((rows, owned), kind),
            pltpu.VMEM((replicas - 1, n_cuts, rows, owned // n_cuts), kind),
            pltpu.VMEM((replicas, rows, heads), kind),
            pltpu.VMEM((width, heads), kind),
            pltpu.VMEM((rows, width), kind),
            pltpu.VMEM((replicas, 8, LANES), jnp.int32),
            pltpu.VMEM(assistant_mask.shape[1:], jnp.int32),
            dma((3,)),
            dma((x_cuts,)),
            dma((replicas, n_cuts)),
            dma((replicas, n_cuts)),
            dma((replicas,)),
            dma((replicas,)),
            dma((replicas, tensors)),
            dma((replicas, tensors)),
            dma((replicas,)),
            dma((replicas,)),
            dma((x_cuts,)),
            dma((x_cuts,)),
        ],
        compiler_params=pltpu.CompilerParams(
            collective_id=0, has_side_effects=True, vmem_limit_bytes=held + (8 << 20)
        ),
        name="exchange",
    )(*arguments)
    out_cuts = pieces_of(owned, LANES, 4)
    return pl.pallas_call(
        functools.partial(finish, out_cuts),
        out_shape=(
            jax.ShapeDtypeStruct((1, 1, owned, heads), jnp.float32),
            jax.ShapeDtypeStruct((1, rows, width), kind),
        ),
        in_specs=[vmem, vmem],
        out_specs=(anywhere, anywhere),
        scratch_shapes=[dma((out_cuts,)), dma((out_cuts,))],
        name="finish",
    )(total, passed)


def with_collectives(normed, w_value, grad_value, assistant_mask):
    local_count = jnp.sum(assistant_mask, dtype=jnp.int32)
    mask_total = lax.psum(local_count, "dp")
    divisor = mask_total.astype(jnp.float32)
    inputs = normed[0]
    weight = w_value[0]
    upstream = grad_value[0]
    local_width = inputs.shape[1]
    replicas = lax.axis_size("dp")
    padded_rows = (local_width + replicas - 1) // replicas * replicas
    padded = jnp.pad(inputs, ((0, 0), (0, padded_rows - local_width)))
    weight_sum = lax.psum_scatter(
        lax.dot_general(
            padded, upstream, (((0,), (0,)), ((), ())), preferred_element_type=jnp.float32
        ).astype(jnp.bfloat16),
        "dp",
        scatter_dimension=0,
        tiled=True,
    ).astype(jnp.float32)
    total = jnp.zeros((upstream.shape[0], local_width), jnp.float32)
    for head in range(KV_HEADS):
        piece_up = upstream[:, head * HEAD : (head + 1) * HEAD]
        piece_w = weight[:, head * HEAD : (head + 1) * HEAD]
        part = lax.dot_general(
            piece_up, piece_w, (((1,), (1,)), ((), ())), preferred_element_type=jnp.float32
        ).astype(jnp.bfloat16)
        total = total + part.astype(jnp.float32)
    weight_grad = weight_sum / divisor
    input_grad = (total / divisor).astype(jnp.bfloat16)
    passed = from_behind(input_grad, "pipe", -1)
    return (weight_grad[None, None], passed[None])


def solution(mesh):
    replicas, tensors, sections = mesh.shape["dp"], mesh.shape["tensor"], mesh.shape["pipe"]

    def local(normed, w_value, grad_value, assistant_mask):
        _, rows, width = normed.shape
        aligned = width % (replicas * LANES) == 0 and rows % (tensors * PACK) == 0
        aligned = aligned and replicas & (replicas - 1) == 0
        if aligned and min(replicas, tensors, sections) > 1:
            return in_kernels(replicas, tensors, sections, normed, w_value, grad_value, assistant_mask)
        return with_collectives(normed, w_value, grad_value, assistant_mask)

    return jax.shard_map(
        local,
        mesh=mesh,
        in_specs=(
            P("pipe", "dp", "tensor"),
            P("pipe", "tensor", None),
            P("pipe", "dp", None),
            P("dp", None, None),
        ),
        out_specs=(P("pipe", "tensor", "dp", None), P("pipe", "dp", "tensor")),
        check_vma=False,
    )
```

time: 119 us -> 112 us (0.941)
  Pallas kernels: 114 us -> 107 us
    pallas_call x1, Pallas kernels: 110 us -> 101 us  [in_kernels(): pl.pallas_call(functools.partial(exchange, replicas, tensors, sections, x...]
    pallas_call x1, Pallas kernels: 3.33 us -> 6.54 us  [in_kernels(): pl.pallas_call(functools.partial(finish, out_cuts), out_shape=(jax.ShapeD...]
    unnamed x6 -> x4, local copies, waits for them, and re-layouts: 4.11 us -> 3.75 us
where the time goes in v2:
time: 112 us; the launch traced here: 111 us
  Pallas kernels  107 us (96%)
  local copies, waits for them, and re-layouts  3.75 us (3%)
    pallas_call x1, Pallas kernels, in_kernels(): pl.pallas_call(functools.partial(exchange, replicas, tensors, sections, x...  101 us
    pallas_call x1, Pallas kernels, in_kernels(): pl.pallas_call(functools.partial(finish, out_cuts), out_shape=(jax.ShapeD...  6.54 us
    unnamed x4, local copies, waits for them, and re-layouts  3.75 us

profile of v2, /device:TPU:0, one launch (start us, length us, event | category | flops | bytes accessed | tf_op | source)
XLA Modules:
  0.0 111.5 jit_solution(10338803500441817871)
XLA Ops:
  0.6 100.6 %exchange.1 = (f32[1024,1024]{1,0:T(8,128)S(1)}, bf16[448,4096]{1,0:T(8,128)(2,1)S(1)}) custom-call(bf16[1,448,4096]{2,1,0:T(8,128)(2,1)} %normed.1, bf16[1,4096,1024]{2,1,0:T(8,128)(2,1)} %weight.1, bf16[1,448,1024]{2,1,0:T(8,128)(2,1)} %grad.1, s32[1,4,8192]{2,1,0:T(4,128)} %mask.1), custom_call_target="tpu_custom_call" | custom-call | tf_op jit(solution)/shard_map/exchange/pallas_call | solution.py:275
  101.2 0.0 copy-start
  101.2 1.9 %copy-done = f32[1024,1024]{1,0:T(8,128)} copy-done((f32[1024,1024]{1,0:T(8,128)}, f32[1024,1024]{1,0:T(8,128)S(1)}, u32[]{:S(2)}) %copy-start) | copy-done | bytes 4194328
  103.1 0.0 copy-start.1
  103.1 1.8 %copy-done.1 = bf16[448,4096]{1,0:T(8,128)(2,1)} copy-done((bf16[448,4096]{1,0:T(8,128)(2,1)}, bf16[448,4096]{1,0:T(8,128)(2,1)S(1)}, u32[]{:S(2)}) %copy-start.1) | copy-done | bytes 3670040
  105.0 6.5 %finish.1 = (f32[1,1,1024,1024]{3,2,1,0:T(8,128)}, bf16[1,448,4096]{2,1,0:T(8,128)(2,1)}) custom-call(f32[1024,1024]{1,0:T(8,128)} %copy-done, bf16[448,4096]{1,0:T(8,128)(2,1)} %copy-done.1), custom_call_target="tpu_custom_call" | custom-call | tf_op jit(solution)/shard_map/finish/pallas_call | solution.py:310
Async XLA Ops:
  101.2 1.9 %copy-start = (f32[1024,1024]{1,0:T(8,128)}, f32[1024,1024]{1,0:T(8,128)S(1)}, u32[]{:S(2)}) copy-start(f32[1024,1024]{1,0:T(8,128)S(1)} %get-tuple-element.4.total) | copy-start | bytes 12582916
  103.1 1.8 %copy-start.1 = (bf16[448,4096]{1,0:T(8,128)(2,1)}, bf16[448,4096]{1,0:T(8,128)(2,1)S(1)}, u32[]{:S(2)}) copy-start(bf16[448,4096]{1,0:T(8,128)(2,1)S(1)} %get-tuple-element.5.passed) | copy-start | bytes 11010052

commit v3 on v2

--- a/solution.py
+++ b/solution.py
@@ -198,15 +198,15 @@
     for k in range(n_cuts):
         cut = slice(k * tile, (k + 1) * tile)
         total[cut, :] = times(mine[:, cut], 0)
+    for k in range(n_cuts - ahead):
+        for d in offsets:
+            n_copies[d, k].wait_send()
+            n_copies[d, k + ahead].start()
     for d in offsets:
         for e in range(1, tensors):
             forwards[d, e].wait_recv()
     for k in range(n_cuts):
         cut = slice(k * tile, (k + 1) * tile)
-        if k + ahead < n_cuts:
-            for d in offsets:
-                n_copies[d, k].wait_send()
-                n_copies[d, k + ahead].start()
         if k == n_cuts - 1:
 
             @pl.when(pipe < sections - 1)
@@ -316,6 +316,7 @@
         in_specs=[vmem, vmem],
         out_specs=(anywhere, anywhere),
         scratch_shapes=[dma((out_cuts,)), dma((out_cuts,))],
+        compiler_params=pltpu.CompilerParams(vmem_limit_bytes=8 << 20),
         name="finish",
     )(total, passed)
 

time: 112 us -> 104 us (0.929)
  Pallas kernels: 107 us -> 103 us
  local copies, waits for them, and re-layouts: 3.75 us -> 0 us
    unnamed x4 -> x0, local copies, waits for them, and re-layouts: 3.75 us -> none
    pallas_call x1, Pallas kernels: 6.54 us -> 3.22 us  [in_kernels(): pl.pallas_call(functools.partial(finish, out_cuts), out_shape=(jax.ShapeD...]
where the time goes in v3:
time: 104 us
  Pallas kernels  103 us (99%)
    pallas_call x1, Pallas kernels, in_kernels(): pl.pallas_call(functools.partial(exchange, replicas, tensors, sections, x...  99.7 us
    pallas_call x1, Pallas kernels, in_kernels(): pl.pallas_call(functools.partial(finish, out_cuts), out_shape=(jax.ShapeD...  3.22 us

profile of v3, /device:TPU:0, one launch (start us, length us, event | category | flops | bytes accessed | tf_op | source)
XLA Modules:
  0.0 103.5 jit_solution(586366527533602570)
XLA Ops:
  0.6 99.7 %exchange.1 = (f32[1024,1024]{1,0:T(8,128)S(1)}, bf16[448,4096]{1,0:T(8,128)(2,1)S(1)}) custom-call(bf16[1,448,4096]{2,1,0:T(8,128)(2,1)} %normed.1, bf16[1,4096,1024]{2,1,0:T(8,128)(2,1)} %weight.1, bf16[1,448,1024]{2,1,0:T(8,128)(2,1)} %grad.1, s32[1,4,8192]{2,1,0:T(4,128)} %mask.1), custom_call_target="tpu_custom_call" | custom-call | tf_op jit(solution)/shard_map/exchange/pallas_call | solution.py:275
  100.3 3.2 %finish.1 = (f32[1,1,1024,1024]{3,2,1,0:T(8,128)}, bf16[1,448,4096]{2,1,0:T(8,128)(2,1)}) custom-call(f32[1024,1024]{1,0:T(8,128)S(1)} %get-tuple-element.4.total, bf16[448,4096]{1,0:T(8,128)(2,1)S(1)} %get-tuple-element.5.passed), custom_call_target="tpu_custom_call" | custom-call | tf_op jit(solution)/shard_map/finish/pallas_call | solution.py:310

commit v4 on v3

--- a/solution.py
+++ b/solution.py
@@ -30,8 +30,8 @@
 def exchange(
     replicas, tensors, sections, x_cuts, n_cuts,
     normed, weight, grad, mask,
-    total, passed,
-    mine, arrived, grads, weights, sending, counts, masks,
+    total, passed, grads, last, scale,
+    mine, arrived, weights, sending, counts, masks,
     load_sem, w_sem, n_send, n_recv, g_send, g_recv, f_send, f_recv, c_send, c_recv, x_send, x_recv,
 ):
     dp = lax.axis_index("dp")
@@ -102,7 +102,7 @@
     def n_copy(d, k):
         return pltpu.make_async_remote_copy(
             src_ref=normed.at[0, :, columns(peer(d), k)],
-            dst_ref=arrived.at[d - 1, k],
+            dst_ref=last.at[d - 1] if k == n_cuts - 1 else arrived.at[d - 1, k],
             send_sem=n_send.at[d, k],
             recv_sem=n_recv.at[d, k],
             device_id={"dp": peer(d)},
@@ -187,7 +187,9 @@
     whole = counts[0]
     for d in offsets:
         whole = whole + counts[d]
-    divisor = whole.astype(jnp.float32)[0:1, 0:1]
+    factor = 1.0 / whole.astype(jnp.float32)
+    scale[...] = factor
+    factor = factor[0:1, 0:1]
 
     def times(block, d):
         return lax.dot_general(
@@ -205,33 +207,33 @@
     for d in offsets:
         for e in range(1, tensors):
             forwards[d, e].wait_recv()
-    for k in range(n_cuts):
+    for k in range(n_cuts - 1):
         cut = slice(k * tile, (k + 1) * tile)
-        if k == n_cuts - 1:
-
-            @pl.when(pipe < sections - 1)
-            def _():
-                for c in range(x_cuts):
-                    x_copy(c).wait_recv()
-                    wide = slice(c * step, (c + 1) * step)
-                    passed[:, wide] = (passed[:, wide].astype(jnp.float32) / divisor).astype(passed.dtype)
-
-            @pl.when(pipe == sections - 1)
-            def _():
-                passed[...] = jnp.zeros(passed.shape, passed.dtype)
-
-            @pl.when(pipe > 0)
-            def _():
-                for c in range(x_cuts):
-                    x_copy(c).wait_send()
-
         for d in reversed(offsets):
             n_copies[d, k].wait_recv()
             if d == offsets[0]:
-                total[cut, :] = (total[cut, :] + times(arrived[d - 1, k], d)) / divisor
+                total[cut, :] = (total[cut, :] + times(arrived[d - 1, k], d)) * factor
             else:
                 total[cut, :] += times(arrived[d - 1, k], d)
 
+    @pl.when(pipe < sections - 1)
+    def _():
+        for c in range(x_cuts):
+            x_copy(c).wait_recv()
+            wide = slice(c * step, (c + 1) * step)
+            passed[:, wide] = (passed[:, wide].astype(jnp.float32) * factor).astype(passed.dtype)
+
+    @pl.when(pipe == sections - 1)
+    def _():
+        passed[...] = jnp.zeros(passed.shape, passed.dtype)
+
+    @pl.when(pipe > 0)
+    def _():
+        for c in range(x_cuts):
+            x_copy(c).wait_send()
+
+    for d in reversed(offsets):
+        n_copies[d, n_cuts - 1].wait_recv()
     for k in range(max(n_cuts - ahead, 0), n_cuts):
         for d in offsets:
             n_copies[d, k].wait_send()
@@ -241,16 +243,29 @@
             forwards[d, e].wait_send()
 
 
-def finish(cuts, total, passed, grad_out, passed_out, g_sem, p_sem):
-    high = total.shape[0] // cuts
+def finish(cuts, total, passed, grads, last, scale, grad_out, passed_out, closing, g_sem, p_sem):
+    high = closing.shape[0]
     wide = passed.shape[1] // cuts
+    ready = total.shape[0] - high
     copies = []
     for c in range(cuts):
-        tall, cut = pl.ds(c * high, high), pl.ds(c * wide, wide)
+        cut = pl.ds(c * wide, wide)
+        copies.append(pltpu.make_async_copy(passed.at[:, cut], passed_out.at[0, :, cut], p_sem.at[c]))
+    for c in range(ready // high):
+        tall = pl.ds(c * high, high)
         copies.append(pltpu.make_async_copy(total.at[tall], grad_out.at[0, 0, tall], g_sem.at[c]))
-        copies.append(pltpu.make_async_copy(passed.at[:, cut], passed_out.at[0, :, cut], p_sem.at[c]))
     for copy in copies:
         copy.start()
+    rest = total[ready:, :]
+    for d in range(1, grads.shape[0]):
+        rest = rest + lax.dot_general(
+            last[d - 1], grads[d], (((0,), (0,)), ((), ())), preferred_element_type=jnp.float32
+        )
+    closing[...] = rest * scale[0:1, 0:1]
+    copies.append(
+        pltpu.make_async_copy(closing, grad_out.at[0, 0, pl.ds(ready, high)], g_sem.at[ready // high])
+    )
+    copies[-1].start()
     for copy in copies:
         copy.wait()
 
@@ -272,18 +287,20 @@
         pltpu.with_memory_space_constraint(array, pltpu.HBM)
         for array in (normed, w_value, grad_value, assistant_mask)
     ]
-    total, passed = pl.pallas_call(
+    results = pl.pallas_call(
         functools.partial(exchange, replicas, tensors, sections, x_cuts, n_cuts),
         out_shape=(
             pltpu.VMEM((owned, heads), jnp.float32),
             pltpu.VMEM((rows, width), kind),
+            pltpu.VMEM((replicas, rows, heads), kind),
+            pltpu.VMEM((replicas - 1, rows, owned // n_cuts), kind),
+            pltpu.VMEM((8, LANES), jnp.float32),
         ),
         in_specs=[anywhere] * 4,
-        out_specs=(vmem, vmem),
+        out_specs=(vmem,) * 5,
         scratch_shapes=[
             pltpu.VMEM((rows, owned), kind),
-            pltpu.VMEM((replicas - 1, n_cuts, rows, owned // n_cuts), kind),
-            pltpu.VMEM((replicas, rows, heads), kind),
+            pltpu.VMEM((replicas - 1, max(n_cuts - 1, 1), rows, owned // n_cuts), kind),
             pltpu.VMEM((width, heads), kind),
             pltpu.VMEM((rows, width), kind),
             pltpu.VMEM((replicas, 8, LANES), jnp.int32),
@@ -306,19 +323,23 @@
         ),
         name="exchange",
     )(*arguments)
-    out_cuts = pieces_of(owned, LANES, 4)
+    out_cuts = pieces_of(width, LANES, 4)
     return pl.pallas_call(
         functools.partial(finish, out_cuts),
         out_shape=(
             jax.ShapeDtypeStruct((1, 1, owned, heads), jnp.float32),
             jax.ShapeDtypeStruct((1, rows, width), kind),
         ),
-        in_specs=[vmem, vmem],
+        in_specs=[vmem] * 5,
         out_specs=(anywhere, anywhere),
-        scratch_shapes=[dma((out_cuts,)), dma((out_cuts,))],
-        compiler_params=pltpu.CompilerParams(vmem_limit_bytes=8 << 20),
+        scratch_shapes=[
+            pltpu.VMEM((owned // n_cuts, heads), jnp.float32),
+            dma((n_cuts,)),
+            dma((out_cuts,)),
+        ],
+        compiler_params=pltpu.CompilerParams(vmem_limit_bytes=4 * owned * heads + (8 << 20)),
         name="finish",
-    )(total, passed)
+    )(*results)
 
 
 def with_collectives(normed, w_value, grad_value, assistant_mask):

time: 104 us -> 103 us (level)
  no operation moved by 1% of the time
where the time goes in v4:
time: 103 us
  Pallas kernels  102 us (99%)
    pallas_call x1, Pallas kernels, in_kernels(): pl.pallas_call(functools.partial(exchange, replicas, tensors, sections, x...  99 us
    pallas_call x1, Pallas kernels, in_kernels(): pl.pallas_call(functools.partial(finish, out_cuts), out_shape=(jax.ShapeD...  3.23 us

profile of v4, /device:TPU:0, one launch (start us, length us, event | category | flops | bytes accessed | tf_op | source)
XLA Modules:
  0.0 102.9 jit_solution(17619450225698535772)
XLA Ops:
  0.6 99.0 %exchange.1 = (f32[1024,1024]{1,0:T(8,128)S(1)}, bf16[448,4096]{1,0:T(8,128)(2,1)S(1)}, bf16[4,448,1024]{2,1,0:T(8,128)(2,1)S(1)}, bf16[3,448,256]{2,1,0:T(8,128)(2,1)S(1)}, f32[8,128]{1,0:T(8,128)S(1)}) custom-call(bf16[1,448,4096]{2,1,0:T(8,128)(2,1)} %normed.1, bf16[1,4096,1024]{2,1,0:T(8,128)(2,1)} %weight.1, bf16[1,448,1024]{2,1,0:T(8,128)(2,1)} %grad.1, ...), custom_call_target="tpu_custom_call" | custom-call | tf_op jit(solution)/shard_map/exchange/pallas_call | solution.py:290
  99.6 3.2 %finish.1 = (f32[1,1,1024,1024]{3,2,1,0:T(8,128)}, bf16[1,448,4096]{2,1,0:T(8,128)(2,1)}) custom-call(f32[1024,1024]{1,0:T(8,128)S(1)} %get-tuple-element.7.total, bf16[448,4096]{1,0:T(8,128)(2,1)S(1)} %get-tuple-element.8.passed, bf16[4,448,1024]{2,1,0:T(8,128)(2,1)S(1)} %get-tuple-element.9.grads, bf16[3,448,256]{2,1,0:T(8,128)(2,1)S(1)} %get-tuple-element.10.last, ...), custom_call_target="tpu_custom_call" | custom-call | tf_op jit(solution)/shard_map/finish/pallas_call | solution.py:327

commit v5 on v4

--- a/solution.py
+++ b/solution.py
@@ -27,11 +27,18 @@
     return 1
 
 
+def spans_of(extent):
+    unit = extent // 8
+    sizes = [unit, 2 * unit, 2 * unit, 2 * unit, unit] if extent % (8 * LANES) == 0 else [extent]
+    starts = [sum(sizes[:i]) for i in range(len(sizes))]
+    return list(zip(starts, sizes))
+
+
 def exchange(
-    replicas, tensors, sections, x_cuts, n_cuts,
+    replicas, tensors, sections, x_cuts, spans, closing,
     normed, weight, grad, mask,
-    total, passed, grads, last, scale,
-    mine, arrived, weights, sending, counts, masks,
+    total, passed, grads, arrived, scale,
+    mine, weights, sending, counts, masks,
     load_sem, w_sem, n_send, n_recv, g_send, g_recv, f_send, f_recv, c_send, c_recv, x_send, x_recv,
 ):
     dp = lax.axis_index("dp")
@@ -40,7 +47,7 @@
     rows = grads.shape[1]
     share = rows // tensors
     owned = mine.shape[1]
-    tile = owned // n_cuts
+    n_cuts = len(spans)
     step = passed.shape[1] // x_cuts
     bits = [1 << b for b in reversed(range(replicas.bit_length() - 1))]
     offsets = range(replicas - 1, 0, -1)
@@ -55,7 +62,7 @@
         return pl.ds(pl.multiple_of(index * share, PACK), share)
 
     def columns(index, k):
-        return pl.ds(pl.multiple_of(index * owned + k * tile, LANES), tile)
+        return pl.ds(pl.multiple_of(index * owned + spans[k][0], LANES), spans[k][1])
 
     barrier = pltpu.get_barrier_semaphore()
     for d in offsets:
@@ -102,7 +109,7 @@
     def n_copy(d, k):
         return pltpu.make_async_remote_copy(
             src_ref=normed.at[0, :, columns(peer(d), k)],
-            dst_ref=last.at[d - 1] if k == n_cuts - 1 else arrived.at[d - 1, k],
+            dst_ref=arrived.at[d - 1, :, pl.ds(*spans[k])],
             send_sem=n_send.at[d, k],
             recv_sem=n_recv.at[d, k],
             device_id={"dp": peer(d)},
@@ -197,8 +204,8 @@
         )
 
     mine_load.wait()
-    for k in range(n_cuts):
-        cut = slice(k * tile, (k + 1) * tile)
+    for start, extent in spans:
+        cut = slice(start, start + extent)
         total[cut, :] = times(mine[:, cut], 0)
     for k in range(n_cuts - ahead):
         for d in offsets:
@@ -207,14 +214,14 @@
     for d in offsets:
         for e in range(1, tensors):
             forwards[d, e].wait_recv()
-    for k in range(n_cuts - 1):
-        cut = slice(k * tile, (k + 1) * tile)
+    for k in range(n_cuts - closing):
+        cut = slice(spans[k][0], spans[k][0] + spans[k][1])
         for d in reversed(offsets):
             n_copies[d, k].wait_recv()
             if d == offsets[0]:
-                total[cut, :] = (total[cut, :] + times(arrived[d - 1, k], d)) * factor
+                total[cut, :] = (total[cut, :] + times(arrived[d - 1, :, cut], d)) * factor
             else:
-                total[cut, :] += times(arrived[d - 1, k], d)
+                total[cut, :] += times(arrived[d - 1, :, cut], d)
 
     @pl.when(pipe < sections - 1)
     def _():
@@ -232,8 +239,9 @@
         for c in range(x_cuts):
             x_copy(c).wait_send()
 
-    for d in reversed(offsets):
-        n_copies[d, n_cuts - 1].wait_recv()
+    for k in range(n_cuts - closing, n_cuts):
+        for d in reversed(offsets):
+            n_copies[d, k].wait_recv()
     for k in range(max(n_cuts - ahead, 0), n_cuts):
         for d in offsets:
             n_copies[d, k].wait_send()
@@ -243,29 +251,33 @@
             forwards[d, e].wait_send()
 
 
-def finish(cuts, total, passed, grads, last, scale, grad_out, passed_out, closing, g_sem, p_sem):
-    high = closing.shape[0]
+def finish(cuts, spans, total, passed, grads, arrived, scale, grad_out, passed_out, rest, g_sem, p_sem):
+    ready = spans[0][0]
     wide = passed.shape[1] // cuts
-    ready = total.shape[0] - high
     copies = []
+    if ready:
+        tall = pl.ds(0, ready)
+        copies.append(pltpu.make_async_copy(total.at[tall], grad_out.at[0, 0, tall], g_sem.at[0]))
     for c in range(cuts):
         cut = pl.ds(c * wide, wide)
         copies.append(pltpu.make_async_copy(passed.at[:, cut], passed_out.at[0, :, cut], p_sem.at[c]))
-    for c in range(ready // high):
-        tall = pl.ds(c * high, high)
-        copies.append(pltpu.make_async_copy(total.at[tall], grad_out.at[0, 0, tall], g_sem.at[c]))
     for copy in copies:
         copy.start()
-    rest = total[ready:, :]
-    for d in range(1, grads.shape[0]):
-        rest = rest + lax.dot_general(
-            last[d - 1], grads[d], (((0,), (0,)), ((), ())), preferred_element_type=jnp.float32
-        )
-    closing[...] = rest * scale[0:1, 0:1]
-    copies.append(
-        pltpu.make_async_copy(closing, grad_out.at[0, 0, pl.ds(ready, high)], g_sem.at[ready // high])
-    )
-    copies[-1].start()
+    for k, (start, extent) in enumerate(spans):
+        cut = slice(start, start + extent)
+        here = pl.ds(start - ready, extent)
+        part = total[cut, :]
+        for d in range(1, grads.shape[0]):
+            part = part + lax.dot_general(
+                arrived[d - 1, :, cut], grads[d], (((0,), (0,)), ((), ())), preferred_element_type=jnp.float32
+            )
+        rest[here, :] = part * scale[0:1, 0:1]
+        copies.append(
+            pltpu.make_async_copy(
+                rest.at[here], grad_out.at[0, 0, pl.ds(start, extent)], g_sem.at[k + 1]
+            )
+        )
+        copies[-1].start()
     for copy in copies:
         copy.wait()
 
@@ -275,7 +287,9 @@
     heads = w_value.shape[2]
     owned = width // replicas
     x_cuts = pieces_of(width, LANES, 8)
-    n_cuts = pieces_of(owned, LANES, 4)
+    spans = spans_of(owned)
+    closing = min(2, len(spans))
+    n_cuts = len(spans)
     kind = normed.dtype
     vmem = pl.BlockSpec(memory_space=pltpu.VMEM)
     anywhere = pl.BlockSpec(memory_space=pl.ANY)
@@ -288,19 +302,18 @@
         for array in (normed, w_value, grad_value, assistant_mask)
     ]
     results = pl.pallas_call(
-        functools.partial(exchange, replicas, tensors, sections, x_cuts, n_cuts),
+        functools.partial(exchange, replicas, tensors, sections, x_cuts, spans, closing),
         out_shape=(
             pltpu.VMEM((owned, heads), jnp.float32),
             pltpu.VMEM((rows, width), kind),
             pltpu.VMEM((replicas, rows, heads), kind),
-            pltpu.VMEM((replicas - 1, rows, owned // n_cuts), kind),
+            pltpu.VMEM((replicas - 1, rows, owned), kind),
             pltpu.VMEM((8, LANES), jnp.float32),
         ),
         in_specs=[anywhere] * 4,
         out_specs=(vmem,) * 5,
         scratch_shapes=[
             pltpu.VMEM((rows, owned), kind),
-            pltpu.VMEM((replicas - 1, max(n_cuts - 1, 1), rows, owned // n_cuts), kind),
             pltpu.VMEM((width, heads), kind),
             pltpu.VMEM((rows, width), kind),
             pltpu.VMEM((replicas, 8, LANES), jnp.int32),
@@ -325,7 +338,7 @@
     )(*arguments)
     out_cuts = pieces_of(width, LANES, 4)
     return pl.pallas_call(
-        functools.partial(finish, out_cuts),
+        functools.partial(finish, out_cuts, spans[-closing:]),
         out_shape=(
             jax.ShapeDtypeStruct((1, 1, owned, heads), jnp.float32),
             jax.ShapeDtypeStruct((1, rows, width), kind),
@@ -333,8 +346,8 @@
         in_specs=[vmem] * 5,
         out_specs=(anywhere, anywhere),
         scratch_shapes=[
-            pltpu.VMEM((owned // n_cuts, heads), jnp.float32),
-            dma((n_cuts,)),
+            pltpu.VMEM((owned - spans[-closing][0], heads), jnp.float32),
+            dma((closing + 1,)),
             dma((out_cuts,)),
         ],
         compiler_params=pltpu.CompilerParams(vmem_limit_bytes=4 * owned * heads + (8 << 20)),

time: 103 us -> 103 us (level)
  no operation moved by 1% of the time
where the time goes in v5:
time: 103 us
  Pallas kernels  102 us (99%)
    pallas_call x1, Pallas kernels, in_kernels(): pl.pallas_call(functools.partial(exchange, replicas, tensors, sections, x...  99.1 us
    pallas_call x1, Pallas kernels, in_kernels(): pl.pallas_call(functools.partial(finish, out_cuts, spans[-closing:]), out...  3.35 us

profile of v5, /device:TPU:0, one launch (start us, length us, event | category | flops | bytes accessed | tf_op | source)
XLA Modules:
  0.0 103.1 jit_solution(7774927930778042049)
XLA Ops:
  0.6 99.1 %exchange.1 = (f32[1024,1024]{1,0:T(8,128)S(1)}, bf16[448,4096]{1,0:T(8,128)(2,1)S(1)}, bf16[4,448,1024]{2,1,0:T(8,128)(2,1)S(1)}, bf16[3,448,1024]{2,1,0:T(8,128)(2,1)S(1)}, f32[8,128]{1,0:T(8,128)S(1)}) custom-call(bf16[1,448,4096]{2,1,0:T(8,128)(2,1)} %normed.1, bf16[1,4096,1024]{2,1,0:T(8,128)(2,1)} %weight.1, bf16[1,448,1024]{2,1,0:T(8,128)(2,1)} %grad.1, ...), custom_call_target="tpu_custom_call" | custom-call | tf_op jit(solution)/shard_map/exchange/pallas_call | solution.py:304
  99.7 3.4 %finish.1 = (f32[1,1,1024,1024]{3,2,1,0:T(8,128)}, bf16[1,448,4096]{2,1,0:T(8,128)(2,1)}) custom-call(f32[1024,1024]{1,0:T(8,128)S(1)} %get-tuple-element.7.total, bf16[448,4096]{1,0:T(8,128)(2,1)S(1)} %get-tuple-element.8.passed, bf16[4,448,1024]{2,1,0:T(8,128)(2,1)S(1)} %get-tuple-element.9.grads, bf16[3,448,1024]{2,1,0:T(8,128)(2,1)S(1)} %get-tuple-element.10.arrived, ...), custom_call_target="tpu_custom_call" | custom-call | tf_op jit(solution)/shard_map/finish/pallas_call | solution.py:340

commit v6 on v4

--- a/solution.py
+++ b/solution.py
@@ -99,13 +99,13 @@
             device_id_type=MESH,
         )
 
-    def n_copy(d, k):
+    def n_copy(target, d, j, k):
         return pltpu.make_async_remote_copy(
-            src_ref=normed.at[0, :, columns(peer(d), k)],
+            src_ref=normed.at[0, :, columns(target, k)],
             dst_ref=last.at[d - 1] if k == n_cuts - 1 else arrived.at[d - 1, k],
-            send_sem=n_send.at[d, k],
+            send_sem=n_send.at[j, k],
             recv_sem=n_recv.at[d, k],
-            device_id={"dp": peer(d)},
+            device_id={"dp": target},
             device_id_type=MESH,
         )
 
@@ -135,10 +135,20 @@
     for b in bits:
         g_copies[b].start()
     ahead = min(2, n_cuts)
-    n_copies = {(d, k): n_copy(d, k) for d in offsets for k in range(n_cuts)}
-    for k in range(ahead):
-        for d in offsets:
-            n_copies[d, k].start()
+    half = replicas // 2
+    upper = dp // half
+    targets = []
+    for i in range(half):
+        target = i * upper + (replicas - 1 - i) * (1 - upper)
+        targets.append((target, sum(b * lax.rem(dp // b + target // b, 2) for b in bits)))
+    targets += [(peer(d), d) for d in range(1, half)]
+    window = [n_cuts] + [ahead] * (len(targets) - 1)
+    sends = {(j, k): n_copy(*targets[j], j, k) for j in range(len(targets)) for k in range(n_cuts)}
+    n_copies = {(d, k): n_copy(peer(d), d, d - 1, k) for d in offsets for k in range(n_cuts)}
+    for k in range(n_cuts):
+        for j in range(len(targets)):
+            if k < window[j]:
+                sends[j, k].start()
 
     grad_load.wait()
 
@@ -201,9 +211,9 @@
         cut = slice(k * tile, (k + 1) * tile)
         total[cut, :] = times(mine[:, cut], 0)
     for k in range(n_cuts - ahead):
-        for d in offsets:
-            n_copies[d, k].wait_send()
-            n_copies[d, k + ahead].start()
+        for j in range(1, len(targets)):
+            sends[j, k].wait_send()
+            sends[j, k + ahead].start()
     for d in offsets:
         for e in range(1, tensors):
             forwards[d, e].wait_recv()
@@ -234,9 +244,9 @@
 
     for d in reversed(offsets):
         n_copies[d, n_cuts - 1].wait_recv()
-    for k in range(max(n_cuts - ahead, 0), n_cuts):
-        for d in offsets:
-            n_copies[d, k].wait_send()
+    for j in range(len(targets)):
+        for k in range(n_cuts - window[j], n_cuts):
+            sends[j, k].wait_send()
     for d in offsets:
         g_copies[d].wait_send()
         for e in range(1, tensors):

time: 103 us -> 103 us (level)
  no operation moved by 1% of the time
where the time goes in v6:
time: 103 us; the launch traced here: 102 us
  Pallas kernels  102 us (99%)
    pallas_call x1, Pallas kernels, in_kernels(): pl.pallas_call(functools.partial(exchange, replicas, tensors, sections, x...  98.5 us
    pallas_call x1, Pallas kernels, in_kernels(): pl.pallas_call(functools.partial(finish, out_cuts), out_shape=(jax.ShapeD...  3.23 us

profile of v6, /device:TPU:0, one launch (start us, length us, event | category | flops | bytes accessed | tf_op | source)
XLA Modules:
  0.0 102.4 jit_solution(17281599439883866117)
XLA Ops:
  0.6 98.5 %exchange.1 = (f32[1024,1024]{1,0:T(8,128)S(1)}, bf16[448,4096]{1,0:T(8,128)(2,1)S(1)}, bf16[4,448,1024]{2,1,0:T(8,128)(2,1)S(1)}, bf16[3,448,256]{2,1,0:T(8,128)(2,1)S(1)}, f32[8,128]{1,0:T(8,128)S(1)}) custom-call(bf16[1,448,4096]{2,1,0:T(8,128)(2,1)} %normed.1, bf16[1,4096,1024]{2,1,0:T(8,128)(2,1)} %weight.1, bf16[1,448,1024]{2,1,0:T(8,128)(2,1)} %grad.1, ...), custom_call_target="tpu_custom_call" | custom-call | tf_op jit(solution)/shard_map/exchange/pallas_call | solution.py:300
  99.1 3.2 %finish.1 = (f32[1,1,1024,1024]{3,2,1,0:T(8,128)}, bf16[1,448,4096]{2,1,0:T(8,128)(2,1)}) custom-call(f32[1024,1024]{1,0:T(8,128)S(1)} %get-tuple-element.7.total, bf16[448,4096]{1,0:T(8,128)(2,1)S(1)} %get-tuple-element.8.passed, bf16[4,448,1024]{2,1,0:T(8,128)(2,1)S(1)} %get-tuple-element.9.grads, bf16[3,448,256]{2,1,0:T(8,128)(2,1)S(1)} %get-tuple-element.10.last, ...), custom_call_target="tpu_custom_call" | custom-call | tf_op jit(solution)/shard_map/finish/pallas_call | solution.py:337

commit v7 on v6

--- a/solution.py
+++ b/solution.py
@@ -28,7 +28,7 @@
 
 
 def exchange(
-    replicas, tensors, sections, x_cuts, n_cuts,
+    replicas, tensors, sections, x_cuts, n_cuts, closing,
     normed, weight, grad, mask,
     total, passed, grads, last, scale,
     mine, arrived, weights, sending, counts, masks,
@@ -41,6 +41,7 @@
     share = rows // tensors
     owned = mine.shape[1]
     tile = owned // n_cuts
+    early = n_cuts - closing
     step = passed.shape[1] // x_cuts
     bits = [1 << b for b in reversed(range(replicas.bit_length() - 1))]
     offsets = range(replicas - 1, 0, -1)
@@ -102,7 +103,7 @@
     def n_copy(target, d, j, k):
         return pltpu.make_async_remote_copy(
             src_ref=normed.at[0, :, columns(target, k)],
-            dst_ref=last.at[d - 1] if k == n_cuts - 1 else arrived.at[d - 1, k],
+            dst_ref=last.at[d - 1, k - early] if k >= early else arrived.at[d - 1, k],
             send_sem=n_send.at[j, k],
             recv_sem=n_recv.at[d, k],
             device_id={"dp": target},
@@ -134,7 +135,7 @@
     g_copies = {b: g_copy(own, 0, b) for b in bits}
     for b in bits:
         g_copies[b].start()
-    ahead = min(2, n_cuts)
+    ahead = min(3, n_cuts)
     half = replicas // 2
     upper = dp // half
     targets = []
@@ -217,7 +218,7 @@
     for d in offsets:
         for e in range(1, tensors):
             forwards[d, e].wait_recv()
-    for k in range(n_cuts - 1):
+    for k in range(early):
         cut = slice(k * tile, (k + 1) * tile)
         for d in reversed(offsets):
             n_copies[d, k].wait_recv()
@@ -242,8 +243,9 @@
         for c in range(x_cuts):
             x_copy(c).wait_send()
 
-    for d in reversed(offsets):
-        n_copies[d, n_cuts - 1].wait_recv()
+    for k in range(early, n_cuts):
+        for d in reversed(offsets):
+            n_copies[d, k].wait_recv()
     for j in range(len(targets)):
         for k in range(n_cuts - window[j], n_cuts):
             sends[j, k].wait_send()
@@ -253,29 +255,33 @@
             forwards[d, e].wait_send()
 
 
-def finish(cuts, total, passed, grads, last, scale, grad_out, passed_out, closing, g_sem, p_sem):
-    high = closing.shape[0]
+def finish(cuts, closing, total, passed, grads, last, scale, grad_out, passed_out, rest, g_sem, p_sem):
+    high = rest.shape[0] // closing
     wide = passed.shape[1] // cuts
-    ready = total.shape[0] - high
+    early = total.shape[0] // high - closing
     copies = []
+    for c in range(early):
+        tall = pl.ds(c * high, high)
+        copies.append(pltpu.make_async_copy(total.at[tall], grad_out.at[0, 0, tall], g_sem.at[c]))
     for c in range(cuts):
         cut = pl.ds(c * wide, wide)
         copies.append(pltpu.make_async_copy(passed.at[:, cut], passed_out.at[0, :, cut], p_sem.at[c]))
-    for c in range(ready // high):
-        tall = pl.ds(c * high, high)
-        copies.append(pltpu.make_async_copy(total.at[tall], grad_out.at[0, 0, tall], g_sem.at[c]))
     for copy in copies:
         copy.start()
-    rest = total[ready:, :]
-    for d in range(1, grads.shape[0]):
-        rest = rest + lax.dot_general(
-            last[d - 1], grads[d], (((0,), (0,)), ((), ())), preferred_element_type=jnp.float32
-        )
-    closing[...] = rest * scale[0:1, 0:1]
-    copies.append(
-        pltpu.make_async_copy(closing, grad_out.at[0, 0, pl.ds(ready, high)], g_sem.at[ready // high])
-    )
-    copies[-1].start()
+    for k in range(closing):
+        c = early + k
+        part = total[c * high : (c + 1) * high, :]
+        for d in range(1, grads.shape[0]):
+            part = part + lax.dot_general(
+                last[d - 1, k], grads[d], (((0,), (0,)), ((), ())), preferred_element_type=jnp.float32
+            )
+        rest[k * high : (k + 1) * high, :] = part * scale[0:1, 0:1]
+        copies.append(
+            pltpu.make_async_copy(
+                rest.at[pl.ds(k * high, high)], grad_out.at[0, 0, pl.ds(c * high, high)], g_sem.at[c]
+            )
+        )
+        copies[-1].start()
     for copy in copies:
         copy.wait()
 
@@ -286,6 +292,7 @@
     owned = width // replicas
     x_cuts = pieces_of(width, LANES, 8)
     n_cuts = pieces_of(owned, LANES, 4)
+    closing = min(2, n_cuts)
     kind = normed.dtype
     vmem = pl.BlockSpec(memory_space=pltpu.VMEM)
     anywhere = pl.BlockSpec(memory_space=pl.ANY)
@@ -298,19 +305,19 @@
         for array in (normed, w_value, grad_value, assistant_mask)
     ]
     results = pl.pallas_call(
-        functools.partial(exchange, replicas, tensors, sections, x_cuts, n_cuts),
+        functools.partial(exchange, replicas, tensors, sections, x_cuts, n_cuts, closing),
         out_shape=(
             pltpu.VMEM((owned, heads), jnp.float32),
             pltpu.VMEM((rows, width), kind),
             pltpu.VMEM((replicas, rows, heads), kind),
-            pltpu.VMEM((replicas - 1, rows, owned // n_cuts), kind),
+            pltpu.VMEM((replicas - 1, closing, rows, owned // n_cuts), kind),
             pltpu.VMEM((8, LANES), jnp.float32),
         ),
         in_specs=[anywhere] * 4,
         out_specs=(vmem,) * 5,
         scratch_shapes=[
             pltpu.VMEM((rows, owned), kind),
-            pltpu.VMEM((replicas - 1, max(n_cuts - 1, 1), rows, owned // n_cuts), kind),
+            pltpu.VMEM((replicas - 1, max(n_cuts - closing, 1), rows, owned // n_cuts), kind),
             pltpu.VMEM((width, heads), kind),
             pltpu.VMEM((rows, width), kind),
             pltpu.VMEM((replicas, 8, LANES), jnp.int32),
@@ -335,7 +342,7 @@
     )(*arguments)
     out_cuts = pieces_of(width, LANES, 4)
     return pl.pallas_call(
-        functools.partial(finish, out_cuts),
+        functools.partial(finish, out_cuts, closing),
         out_shape=(
             jax.ShapeDtypeStruct((1, 1, owned, heads), jnp.float32),
             jax.ShapeDtypeStruct((1, rows, width), kind),
@@ -343,7 +350,7 @@
         in_specs=[vmem] * 5,
         out_specs=(anywhere, anywhere),
         scratch_shapes=[
-            pltpu.VMEM((owned // n_cuts, heads), jnp.float32),
+            pltpu.VMEM((closing * (owned // n_cuts), heads), jnp.float32),
             dma((n_cuts,)),
             dma((out_cuts,)),
         ],

time: 103 us -> 104 us (level)
    pallas_call x1, Pallas kernels: 3.23 us -> 4.34 us  [in_kernels(): pl.pallas_call(functools.partial(finish, out_cuts, closing), out_shape=(j...]
where the time goes in v7:
time: 104 us; the launch traced here: 103 us
  Pallas kernels  103 us (99%)
    pallas_call x1, Pallas kernels, in_kernels(): pl.pallas_call(functools.partial(exchange, replicas, tensors, sections, x...  98.5 us
    pallas_call x1, Pallas kernels, in_kernels(): pl.pallas_call(functools.partial(finish, out_cuts, closing), out_shape=(j...  4.34 us

profile of v7, /device:TPU:0, one launch (start us, length us, event | category | flops | bytes accessed | tf_op | source)
XLA Modules:
  0.0 103.5 jit_solution(4976677361938026857)
XLA Ops:
  0.6 98.5 %exchange.1 = (f32[1024,1024]{1,0:T(8,128)S(1)}, bf16[448,4096]{1,0:T(8,128)(2,1)S(1)}, bf16[4,448,1024]{2,1,0:T(8,128)(2,1)S(1)}, bf16[3,2,448,256]{3,2,1,0:T(8,128)(2,1)S(1)}, f32[8,128]{1,0:T(8,128)S(1)}) custom-call(bf16[1,448,4096]{2,1,0:T(8,128)(2,1)} %normed.1, bf16[1,4096,1024]{2,1,0:T(8,128)(2,1)} %weight.1, bf16[1,448,1024]{2,1,0:T(8,128)(2,1)} %grad.1, ...), custom_call_target="tpu_custom_call" | custom-call | tf_op jit(solution)/shard_map/exchange/pallas_call | solution.py:307
  99.1 4.3 %finish.1 = (f32[1,1,1024,1024]{3,2,1,0:T(8,128)}, bf16[1,448,4096]{2,1,0:T(8,128)(2,1)}) custom-call(f32[1024,1024]{1,0:T(8,128)S(1)} %get-tuple-element.7.total, bf16[448,4096]{1,0:T(8,128)(2,1)S(1)} %get-tuple-element.8.passed, bf16[4,448,1024]{2,1,0:T(8,128)(2,1)S(1)} %get-tuple-element.9.grads, bf16[3,2,448,256]{3,2,1,0:T(8,128)(2,1)S(1)} %get-tuple-element.10.last, ...), custom_call_target="tpu_custom_call" | custom-call | tf_op jit(solution)/shard_map/finish/pallas_call | solution.py:344

commit v8 on v6

--- a/solution.py
+++ b/solution.py
@@ -142,7 +142,7 @@
         target = i * upper + (replicas - 1 - i) * (1 - upper)
         targets.append((target, sum(b * lax.rem(dp // b + target // b, 2) for b in bits)))
     targets += [(peer(d), d) for d in range(1, half)]
-    window = [n_cuts] + [ahead] * (len(targets) - 1)
+    window = [n_cuts] + [ahead] * (half - 1) + [1] * (half - 1)
     sends = {(j, k): n_copy(*targets[j], j, k) for j in range(len(targets)) for k in range(n_cuts)}
     n_copies = {(d, k): n_copy(peer(d), d, d - 1, k) for d in offsets for k in range(n_cuts)}
     for k in range(n_cuts):
@@ -210,10 +210,11 @@
     for k in range(n_cuts):
         cut = slice(k * tile, (k + 1) * tile)
         total[cut, :] = times(mine[:, cut], 0)
-    for k in range(n_cuts - ahead):
-        for j in range(1, len(targets)):
-            sends[j, k].wait_send()
-            sends[j, k + ahead].start()
+    for k in range(n_cuts):
+        for j in range(len(targets)):
+            if k + window[j] < n_cuts:
+                sends[j, k].wait_send()
+                sends[j, k + window[j]].start()
     for d in offsets:
         for e in range(1, tensors):
             forwards[d, e].wait_recv()

time: 103 us -> 107 us (1.039)
  Pallas kernels: 102 us -> 107 us
    pallas_call x1, Pallas kernels: 98.5 us -> 103 us  [in_kernels(): pl.pallas_call(functools.partial(exchange, replicas, tensors, sections, x...]
where the time goes in v8:
time: 107 us
  Pallas kernels  107 us (100%)
    pallas_call x1, Pallas kernels, in_kernels(): pl.pallas_call(functools.partial(exchange, replicas, tensors, sections, x...  103 us
    pallas_call x1, Pallas kernels, in_kernels(): pl.pallas_call(functools.partial(finish, out_cuts), out_shape=(jax.ShapeD...  3.23 us

profile of v8, /device:TPU:0, one launch (start us, length us, event | category | flops | bytes accessed | tf_op | source)
XLA Modules:
  0.0 107.3 jit_solution(13409200581782330521)
XLA Ops:
  0.6 103.4 %exchange.1 = (f32[1024,1024]{1,0:T(8,128)S(1)}, bf16[448,4096]{1,0:T(8,128)(2,1)S(1)}, bf16[4,448,1024]{2,1,0:T(8,128)(2,1)S(1)}, bf16[3,448,256]{2,1,0:T(8,128)(2,1)S(1)}, f32[8,128]{1,0:T(8,128)S(1)}) custom-call(bf16[1,448,4096]{2,1,0:T(8,128)(2,1)} %normed.1, bf16[1,4096,1024]{2,1,0:T(8,128)(2,1)} %weight.1, bf16[1,448,1024]{2,1,0:T(8,128)(2,1)} %grad.1, ...), custom_call_target="tpu_custom_call" | custom-call | tf_op jit(solution)/shard_map/exchange/pallas_call | solution.py:301
  104.0 3.2 %finish.1 = (f32[1,1,1024,1024]{3,2,1,0:T(8,128)}, bf16[1,448,4096]{2,1,0:T(8,128)(2,1)}) custom-call(f32[1024,1024]{1,0:T(8,128)S(1)} %get-tuple-element.7.total, bf16[448,4096]{1,0:T(8,128)(2,1)S(1)} %get-tuple-element.8.passed, bf16[4,448,1024]{2,1,0:T(8,128)(2,1)S(1)} %get-tuple-element.9.grads, bf16[3,448,256]{2,1,0:T(8,128)(2,1)S(1)} %get-tuple-element.10.last, ...), custom_call_target="tpu_custom_call" | custom-call | tf_op jit(solution)/shard_map/finish/pallas_call | solution.py:338
